TPU v7x, 512 devices: a whole 4x8x8 slice. The times are simulated.
512 devices in a mesh: dom: 64 (over y, x, core), col: 8 (over z).
Axes of the slice: x: 4, y: 8, z: 8, core: 2. Of those that a mesh axis runs over, the one named last changes fastest.
Arguments:
- matrix: float32 [1024, 8, 128, 128], P(('dom', 'col'))
- left_slots: int32 [1024, 8, 4], P(('dom', 'col')), may hold values from 0 to 3
- right_rows: int32 [1024, 8, 4], P(('dom', 'col')), may hold values from 0 to 1023, as said below
- right_slots: int32 [1024, 8, 4], P(('dom', 'col')), may hold values from 0 to 3
- pair_counts: int32 [1024, 8], P(('dom', 'col')), may hold values from 0 to 4
- diag_rows: int32 [1024, 4], P(('dom', 'col')), may hold values from 0 to 1023, as said below
Outputs:
- factors: float32 [1024, 8, 128, 128], P(('dom', 'col'))
Inputs may be any that keep to these rules, and one draw needn't show every extreme that they name: With d the domain of row i at grid place (a, b): right_rows[i, s, p] is a row of domain d, or of the last 1 row of the domain at (a - 1, b) or (a, b - 1), or of the first 1 row of the domain at (a + 1, b) or (a, b + 1), where that domain exists. diag_rows[i, s] obeys the same rule as right_rows.
All inputs are finite; a program needn't handle non-finite values.
Results may differ from a plain program's by a relative error of at most 0.0003.
Values sent between devices are 32-bit elements; how exact they have to be, the bound alone decides.
A program may use at most 64 MiB of HBM per device.

v0:
```python
import functools

import jax
import jax.numpy as jnp
from jax import lax
from jax.experimental import pallas as pl
from jax.experimental.pallas import tpu as pltpu
from jax.sharding import PartitionSpec as P

LOWER = 4
UPPER = 4
SLOTS = 8
PAIRS = 4
ROWS = 2
BLOCK = 128
NEWTON_STEPS = 4
OWN, FIRST, SECOND = 0, 1, 2
WINDOW = 3 * UPPER * 2
LEFTS = ROWS * LOWER
MESH = pl.DeviceIdType.MESH
F32, BF16 = jnp.float32, jnp.bfloat16


def split(value):
    high = value.astype(BF16)
    return high, (value - high.astype(F32)).astype(BF16)


def as_left(value):
    high, low = split(value)
    return jnp.concatenate([high, low, high], axis=1)


def as_right(value):
    high, low = split(value)
    return jnp.concatenate([high, high, low], axis=0)


def product(left, right):
    return jnp.dot(left, right, preferred_element_type=F32)


def newton_inverses(squares):
    rows = lax.broadcasted_iota(jnp.int32, (BLOCK, BLOCK), 0)
    columns = lax.broadcasted_iota(jnp.int32, (BLOCK, BLOCK), 1)
    on_diagonal = rows == columns
    identity = jnp.where(on_diagonal, 1.0, 0.0).astype(F32)
    errors, approxes = [], []
    for square in squares:
        diagonal = jnp.where(on_diagonal, square, 0.0)
        error = identity - square * (1.0 / jnp.sum(diagonal, axis=0, keepdims=True))
        errors.append(error)
        approxes.append((identity + error) * (1.0 / jnp.sum(diagonal, axis=1, keepdims=True)))
    errors = [product(as_left(error), as_right(error)) for error in errors]
    for step in range(1, NEWTON_STEPS):
        for index, (error, approx) in enumerate(zip(errors, approxes)):
            right = as_right(error)
            if step < NEWTON_STEPS - 1:
                both = product(as_left(jnp.concatenate([approx, error], axis=0)), right)
                approxes[index] = approx + both[:BLOCK]
                errors[index] = both[BLOCK:]
            else:
                approxes[index] = approx + product(as_left(approx), right)
    return approxes


def kernel(
    matrix_ref, left_hbm, rows_hbm, slots_hbm, counts_hbm, diag_hbm, out_ref,
    left_ref, rows_ref, slots_ref, counts_ref, diag_ref,
    held, lower, upper, halo, products, inverses, places, diag_places,
    load_sem, table_sem, send_sem, recv_sem,
):
    dom, col = lax.axis_index("dom"), lax.axis_index("col")
    doms, cols = lax.axis_size("dom"), lax.axis_size("col")
    own_domain = dom * cols + col
    neighbours = {FIRST: [(dom + 1, col), (dom - 1, col)], SECOND: [(dom, col + 1), (dom, col - 1)]}
    exists = {FIRST: [dom < doms - 1, dom > 0], SECOND: [col < cols - 1, col > 0]}

    def transfer(sweep, kind, e, slot):
        source = matrix_ref.at[1 - e, LOWER + slot] if sweep == 0 else upper.at[1 - e, slot]
        return pltpu.make_async_remote_copy(
            src_ref=source,
            dst_ref=halo.at[sweep, kind - 1, slot, e],
            send_sem=send_sem.at[sweep, kind - 1, slot, e],
            recv_sem=recv_sem.at[sweep, kind - 1, slot, e],
            device_id=neighbours[kind][e],
            device_id_type=MESH,
        )

    def start(sweep, kind, e, slot):
        @pl.when(exists[kind][e])
        def _():
            transfer(sweep, kind, e, slot).start()

    barrier = pltpu.get_barrier_semaphore()
    arrivals = 0
    for kind in (SECOND, FIRST):
        for e in range(2):
            @pl.when(exists[kind][e])
            def _():
                pl.semaphore_signal(
                    barrier, inc=1, device_id=neighbours[kind][e], device_id_type=MESH
                )
            arrivals = arrivals + exists[kind][e].astype(jnp.int32)
    load = pltpu.make_async_copy(matrix_ref, held, load_sem)
    load.start()
    tables = [
        pltpu.make_async_copy(source, target, table_sem.at[index])
        for index, (source, target) in enumerate(
            [
                (left_hbm, left_ref), (rows_hbm, rows_ref), (slots_hbm, slots_ref),
                (counts_hbm, counts_ref), (diag_hbm, diag_ref),
            ]
        )
    ]
    for table in tables:
        table.start()
    pl.semaphore_wait(barrier, arrivals)

    @pl.loop(0, UPPER)
    def _(slot):
        for kind in (SECOND, FIRST):
            for e in range(2):
                start(0, kind, e, slot)

    for kind in (FIRST, SECOND):
        for e in range(2):
            @pl.when(jnp.logical_not(exists[kind][1 - e]))
            def _():
                for sweep in range(2):
                    for slot in range(UPPER):
                        halo[sweep, kind - 1, slot, e] = jnp.zeros((BLOCK, BLOCK), F32)

    for table in tables:
        table.wait()

    def place_of(row):
        shift = lax.shift_right_arithmetic(row, 1) - own_domain
        own = shift == 0
        kind = jnp.where(own, OWN, jnp.where(jnp.abs(shift) == cols, FIRST, SECOND))
        e = jnp.where(own, lax.bitwise_and(row, 1), jnp.where(shift < 0, 0, 1))
        return kind, e

    @pl.loop(0, ROWS * SLOTS)
    def _(target):
        row, slot = lax.div(target, SLOTS), lax.rem(target, SLOTS)
        count = counts_ref[row, slot]
        for pair in range(PAIRS):
            kind, e = place_of(rows_ref[row, pair, slot])
            window = (kind * UPPER + slots_ref[row, pair, slot]) * 2 + e
            place = window * LEFTS + row * LOWER + left_ref[row, pair, slot]
            places[target * PAIRS + pair] = jnp.where(pair < count, place, WINDOW * LEFTS)

    @pl.loop(0, LEFTS)
    def _(target):
        kind, e = place_of(diag_ref[lax.div(target, LOWER), lax.rem(target, LOWER)])
        diag_places[target] = kind * 2 + e

    products[WINDOW * LEFTS] = jnp.zeros((BLOCK, BLOCK), F32)
    load.wait()

    @pl.loop(0, LEFTS)
    def _(index):
        lower[pl.ds(pl.multiple_of(index * BLOCK, BLOCK), BLOCK)] = as_left(
            held[lax.div(index, LOWER), lax.rem(index, LOWER)]
        )

    def multiply(kind, slot, first, second):
        right = jnp.concatenate([as_right(first), as_right(second)], axis=1)
        both = product(lower[...], right).reshape(LEFTS, BLOCK, 2 * BLOCK)
        start = (kind * UPPER + slot) * 2 * LEFTS
        products[pl.ds(start, LEFTS)] = both[:, :, :BLOCK]
        products[pl.ds(start + LEFTS, LEFTS)] = both[:, :, BLOCK:]

    def multiply_halo(sweep, kind, slot):
        for e in range(2):
            @pl.when(exists[kind][1 - e])
            def _():
                transfer(sweep, kind, e, slot).wait_recv()
        multiply(kind, slot, halo[sweep, kind - 1, slot, 0], halo[sweep, kind - 1, slot, 1])

    def fill(sweep):
        def own(row, slot):
            return held[row, LOWER + slot] if sweep == 0 else upper[row, slot]

        for slot in range(UPPER):
            multiply(OWN, slot, own(0, slot), own(1, slot))

        multiply_halo(sweep, FIRST, 0)
        multiply_halo(sweep, SECOND, 0)
        squares = [own(0, 0), own(1, 0)]
        for kind in (FIRST, SECOND):
            squares += [halo[sweep, kind - 1, 0, e] for e in range(2)]
        for index, inverse in enumerate(newton_inverses(squares)):
            inverses[index] = as_right(inverse)

        for slot in range(1, UPPER):
            multiply_halo(sweep, FIRST, slot)
            multiply_halo(sweep, SECOND, slot)

    def residue(row, slot):
        target = (row * SLOTS + slot) * PAIRS
        terms = [products[places[target + pair]] for pair in range(PAIRS)]
        return held[row, slot] - ((terms[0] + terms[1]) + (terms[2] + terms[3]))

    def lower_block(index):
        row, slot = index // LOWER, index % LOWER
        return product(as_left(residue(row, slot)), inverses[diag_places[index]])

    fill(0)

    @pl.loop(0, UPPER)
    def _(slot):
        for row in range(ROWS):
            upper[row, slot] = residue(row, LOWER + slot)
            for kind in (SECOND, FIRST):
                start(1, kind, 1 - row, slot)

    for index in range(LEFTS):
        lower[pl.ds(index * BLOCK, BLOCK)] = as_left(lower_block(index))

    fill(1)

    @pl.loop(0, UPPER)
    def _(slot):
        for row in range(ROWS):
            out_ref[row, LOWER + slot] = residue(row, LOWER + slot)

    for index in range(LEFTS):
        out_ref[index // LOWER, index % LOWER] = lower_block(index)

    @pl.loop(0, UPPER)
    def _(slot):
        for sweep in range(2):
            for kind in (SECOND, FIRST):
                for e in range(2):
                    @pl.when(exists[kind][e])
                    def _():
                        transfer(sweep, kind, e, slot).wait_send()


def local(matrix, left_slots, right_rows, right_slots, pair_counts, diag_rows):
    operands = [matrix]
    operands += [jnp.swapaxes(table, 1, 2) for table in (left_slots, right_rows, right_slots)]
    operands += [pair_counts, diag_rows]
    return pl.pallas_call(
        kernel,
        out_shape=pltpu.VMEM(matrix.shape, F32),
        in_specs=[pl.BlockSpec(memory_space=pltpu.HBM)] * 6,
        out_specs=pl.BlockSpec(memory_space=pltpu.VMEM),
        scratch_shapes=[
            pltpu.SMEM((ROWS, PAIRS, SLOTS), jnp.int32),
            pltpu.SMEM((ROWS, PAIRS, SLOTS), jnp.int32),
            pltpu.SMEM((ROWS, PAIRS, SLOTS), jnp.int32),
            pltpu.SMEM((ROWS, SLOTS), jnp.int32),
            pltpu.SMEM((ROWS, LOWER), jnp.int32),
            pltpu.VMEM((ROWS, SLOTS, BLOCK, BLOCK), F32),
            pltpu.VMEM((LEFTS * BLOCK, 3 * BLOCK), BF16),
            pltpu.VMEM((ROWS, UPPER, BLOCK, BLOCK), F32),
            pltpu.VMEM((2, 2, UPPER, 2, BLOCK, BLOCK), F32),
            pltpu.VMEM((WINDOW * LEFTS + 1, BLOCK, BLOCK), F32),
            pltpu.VMEM((6, 3 * BLOCK, BLOCK), BF16),
            pltpu.SMEM((ROWS * SLOTS * PAIRS,), jnp.int32),
            pltpu.SMEM((LEFTS,), jnp.int32),
            pltpu.SemaphoreType.DMA,
            pltpu.SemaphoreType.DMA((5,)),
            pltpu.SemaphoreType.DMA((2, 2, UPPER, 2)),
            pltpu.SemaphoreType.DMA((2, 2, UPPER, 2)),
        ],
        compiler_params=pltpu.CompilerParams(
            collective_id=0, has_side_effects=True, vmem_limit_bytes=48 * 2**20
        ),
    )(*(pltpu.with_memory_space_constraint(operand, pltpu.HBM) for operand in operands))


def solution(mesh):
    split_rows = ("dom", "col")
    return jax.shard_map(
        local,
        mesh=mesh,
        in_specs=(
            P(split_rows, None, None, None),
            P(split_rows, None, None),
            P(split_rows, None, None),
            P(split_rows, None, None),
            P(split_rows, None),
            P(split_rows, None),
        ),
        out_specs=P(split_rows, None, None, None),
        check_vma=False,
    )
```

profile of v0, /device:TPU:184, one launch (start us, length us, event | category | flops | bytes accessed | tf_op | source)
XLA Modules:
  0.0 29.6 jit_solution(4055121649201957738)
XLA Ops:
  0.0 28.6 %shard_map.64 = f32[2,8,128,128]{3,2,1,0:T(8,128)S(1)} custom-call(f32[2,8,128,128]{3,2,1,0:T(8,128)} %matrix_ref.1, s32[2,4,8]{2,1,0:T(4,128)} %bitcast.3, s32[2,4,8]{2,1,0:T(4,128)} %bitcast.4, s32[2,4,8]{2,1,0:T(4,128)} %bitcast.5, s32[2,8]{1,0:T(2,128)} %counts_hbm.1, s32[2,4]{1,0:T(2,128)} %diag_hbm.1), custom_call_target="tpu_custom_call" | custom-call | tf_op jit(solution)/shard_map/pallas_call | solution.py:246
  28.6 1.0 %copy.8 = f32[2,8,128,128]{3,2,1,0:T(8,128)} copy(f32[2,8,128,128]{3,2,1,0:T(8,128)S(1)} %shard_map.64) | data formatting | bytes 2097152
where the time goes:
time: 29.7 us; the launch traced here: 29.6 us
  Pallas kernels  28.6 us (96%)
  local copies, waits for them, and re-layouts  0.97 us (3%)
    pallas_call x1, Pallas kernels, local(): pl.pallas_call(kernel, out_shape=pltpu.VMEM(matrix.shape, F32), in_specs=...  28.6 us
    unnamed x1, local copies, waits for them, and re-layouts  0.97 us

commit v1 on v0

--- a/solution.py
+++ b/solution.py
@@ -129,7 +129,11 @@
             def _():
                 for sweep in range(2):
                     for slot in range(UPPER):
-                        halo[sweep, kind - 1, slot, e] = jnp.zeros((BLOCK, BLOCK), F32)
+                        pltpu.make_async_copy(
+                            matrix_ref.at[0, LOWER + slot],
+                            halo.at[sweep, kind - 1, slot, e],
+                            recv_sem.at[sweep, kind - 1, slot, e],
+                        ).start()
 
     for table in tables:
         table.wait()
@@ -172,12 +176,20 @@
         products[pl.ds(start, LEFTS)] = both[:, :, :BLOCK]
         products[pl.ds(start + LEFTS, LEFTS)] = both[:, :, BLOCK:]
 
-    def multiply_halo(sweep, kind, slot):
-        for e in range(2):
-            @pl.when(exists[kind][1 - e])
-            def _():
+    def multiply_halo(sweep, *steps):
+        for kind, slot in steps:
+            for e in range(2):
                 transfer(sweep, kind, e, slot).wait_recv()
-        multiply(kind, slot, halo[sweep, kind - 1, slot, 0], halo[sweep, kind - 1, slot, 1])
+        for kind, slot in steps:
+            multiply(kind, slot, halo[sweep, kind - 1, slot, 0], halo[sweep, kind - 1, slot, 1])
+
+    def wait_sent(sweep, slots):
+        for slot in slots:
+            for kind in (FIRST, SECOND):
+                for e in range(2):
+                    @pl.when(exists[kind][e])
+                    def _():
+                        transfer(sweep, kind, e, slot).wait_send()
 
     def fill(sweep):
         def own(row, slot):
@@ -185,18 +197,19 @@
 
         for slot in range(UPPER):
             multiply(OWN, slot, own(0, slot), own(1, slot))
-
-        multiply_halo(sweep, FIRST, 0)
-        multiply_halo(sweep, SECOND, 0)
+        if sweep == 1:
+            wait_sent(0, range(UPPER))
+        multiply_halo(sweep, (FIRST, 0), (SECOND, 0))
         squares = [own(0, 0), own(1, 0)]
         for kind in (FIRST, SECOND):
             squares += [halo[sweep, kind - 1, 0, e] for e in range(2)]
         for index, inverse in enumerate(newton_inverses(squares)):
             inverses[index] = as_right(inverse)
-
-        for slot in range(1, UPPER):
-            multiply_halo(sweep, FIRST, slot)
-            multiply_halo(sweep, SECOND, slot)
+        multiply_halo(sweep, (FIRST, 1), (FIRST, 2), (SECOND, 1))
+        multiply_halo(sweep, (FIRST, 3), (SECOND, 2))
+        if sweep == 1:
+            wait_sent(1, range(UPPER - 1))
+        multiply_halo(sweep, (SECOND, 3))
 
     def residue(row, slot):
         target = (row * SLOTS + slot) * PAIRS
@@ -208,35 +221,24 @@
         return product(as_left(residue(row, slot)), inverses[diag_places[index]])
 
     fill(0)
-
-    @pl.loop(0, UPPER)
-    def _(slot):
-        for row in range(ROWS):
-            upper[row, slot] = residue(row, LOWER + slot)
+    for slots in ((0,), (1, 2, 3)):
+        for slot in slots:
+            for row in range(ROWS):
+                upper[row, slot] = residue(row, LOWER + slot)
+        for slot in slots:
             for kind in (SECOND, FIRST):
-                start(1, kind, 1 - row, slot)
-
+                for e in range(2):
+                    start(1, kind, e, slot)
     for index in range(LEFTS):
         lower[pl.ds(index * BLOCK, BLOCK)] = as_left(lower_block(index))
 
     fill(1)
-
-    @pl.loop(0, UPPER)
-    def _(slot):
+    for index in range(LEFTS):
+        out_ref[index // LOWER, index % LOWER] = lower_block(index)
+    for slot in range(UPPER):
         for row in range(ROWS):
             out_ref[row, LOWER + slot] = residue(row, LOWER + slot)
-
-    for index in range(LEFTS):
-        out_ref[index // LOWER, index % LOWER] = lower_block(index)
-
-    @pl.loop(0, UPPER)
-    def _(slot):
-        for sweep in range(2):
-            for kind in (SECOND, FIRST):
-                for e in range(2):
-                    @pl.when(exists[kind][e])
-                    def _():
-                        transfer(sweep, kind, e, slot).wait_send()
+    wait_sent(1, (UPPER - 1,))
 
 
 def local(matrix, left_slots, right_rows, right_slots, pair_counts, diag_rows):

time: 29.7 us -> 26 us (0.88)
  the two profiles are of different devices: /device:TPU:184 before, /device:TPU:168 now
where the time goes in v1:
time: 26 us; the launch traced here: 25.9 us
  Pallas kernels  24.9 us (96%)
  local copies, waits for them, and re-layouts  0.97 us (4%)
    pallas_call x1, Pallas kernels, local(): pl.pallas_call(kernel, out_shape=pltpu.VMEM(matrix.shape, F32), in_specs=...  24.9 us
    unnamed x1, local copies, waits for them, and re-layouts  0.97 us

profile of v1, /device:TPU:168, one launch (start us, length us, event | category | flops | bytes accessed | tf_op | source)
XLA Modules:
  0.0 25.9 jit_solution(8195050742535619248)
XLA Ops:
  0.0 24.9 %shard_map.64 = f32[2,8,128,128]{3,2,1,0:T(8,128)S(1)} custom-call(f32[2,8,128,128]{3,2,1,0:T(8,128)} %matrix_ref.1, s32[2,4,8]{2,1,0:T(4,128)} %bitcast.3, s32[2,4,8]{2,1,0:T(4,128)} %bitcast.4, s32[2,4,8]{2,1,0:T(4,128)} %bitcast.5, s32[2,8]{1,0:T(2,128)} %counts_hbm.1, s32[2,4]{1,0:T(2,128)} %diag_hbm.1), custom_call_target="tpu_custom_call" | custom-call | tf_op jit(solution)/shard_map/pallas_call | solution.py:248
  24.9 1.0 %copy.8 = f32[2,8,128,128]{3,2,1,0:T(8,128)} copy(f32[2,8,128,128]{3,2,1,0:T(8,128)S(1)} %shard_map.64) | data formatting | bytes 2097152

commit v2 on v1

--- a/solution.py
+++ b/solution.py
@@ -67,7 +67,7 @@
 def kernel(
     matrix_ref, left_hbm, rows_hbm, slots_hbm, counts_hbm, diag_hbm, out_ref,
     left_ref, rows_ref, slots_ref, counts_ref, diag_ref,
-    held, lower, upper, halo, products, inverses, places, diag_places,
+    held, lower, rights, upper, halo, products, inverses, places, diag_places,
     load_sem, table_sem, send_sem, recv_sem,
 ):
     dom, col = lax.axis_index("dom"), lax.axis_index("col")
@@ -77,20 +77,41 @@
     exists = {FIRST: [dom < doms - 1, dom > 0], SECOND: [col < cols - 1, col > 0]}
 
     def transfer(sweep, kind, e, slot):
-        source = matrix_ref.at[1 - e, LOWER + slot] if sweep == 0 else upper.at[1 - e, slot]
+        source = held.at[1 - e, LOWER + slot] if sweep == 0 else upper.at[1 - e, slot]
         return pltpu.make_async_remote_copy(
             src_ref=source,
             dst_ref=halo.at[sweep, kind - 1, slot, e],
-            send_sem=send_sem.at[sweep, kind - 1, slot, e],
-            recv_sem=recv_sem.at[sweep, kind - 1, slot, e],
+            send_sem=send_sem.at[kind - 1, e],
+            recv_sem=recv_sem.at[sweep, kind - 1, slot],
             device_id=neighbours[kind][e],
             device_id_type=MESH,
         )
 
-    def start(sweep, kind, e, slot):
-        @pl.when(exists[kind][e])
-        def _():
-            transfer(sweep, kind, e, slot).start()
+    def send(sweep, slots=range(UPPER)):
+        for kind in (SECOND, FIRST):
+            after, before = exists[kind]
+            for ways, here in (
+                ((0, 1), jnp.logical_and(after, before)),
+                ((0,), jnp.logical_not(before)),
+                ((1,), jnp.logical_not(after)),
+            ):
+                @pl.when(here)
+                def _():
+                    for slot in slots:
+                        for e in ways:
+                            transfer(sweep, kind, e, slot).start()
+
+    def wait_arrived(sweep, kind, slot):
+        place = halo.at[sweep, kind - 1, slot]
+        pltpu.make_async_copy(place, place, recv_sem.at[sweep, kind - 1, slot]).wait()
+
+    def wait_sent():
+        for kind in (FIRST, SECOND):
+            for e in range(2):
+                @pl.when(exists[kind][e])
+                def _():
+                    sent = halo.at[:, kind - 1, :, e]
+                    pltpu.make_async_copy(sent, sent, send_sem.at[kind - 1, e]).wait()
 
     barrier = pltpu.get_barrier_semaphore()
     arrivals = 0
@@ -116,12 +137,9 @@
     for table in tables:
         table.start()
     pl.semaphore_wait(barrier, arrivals)
-
-    @pl.loop(0, UPPER)
-    def _(slot):
-        for kind in (SECOND, FIRST):
-            for e in range(2):
-                start(0, kind, e, slot)
+    load.wait()
+
+    send(0)
 
     for kind in (FIRST, SECOND):
         for e in range(2):
@@ -132,7 +150,7 @@
                         pltpu.make_async_copy(
                             matrix_ref.at[0, LOWER + slot],
                             halo.at[sweep, kind - 1, slot, e],
-                            recv_sem.at[sweep, kind - 1, slot, e],
+                            recv_sem.at[sweep, kind - 1, slot],
                         ).start()
 
     for table in tables:
@@ -161,7 +179,6 @@
         diag_places[target] = kind * 2 + e
 
     products[WINDOW * LEFTS] = jnp.zeros((BLOCK, BLOCK), F32)
-    load.wait()
 
     @pl.loop(0, LEFTS)
     def _(index):
@@ -169,47 +186,54 @@
             held[lax.div(index, LOWER), lax.rem(index, LOWER)]
         )
 
-    def multiply(kind, slot, first, second):
-        right = jnp.concatenate([as_right(first), as_right(second)], axis=1)
-        both = product(lower[...], right).reshape(LEFTS, BLOCK, 2 * BLOCK)
-        start = (kind * UPPER + slot) * 2 * LEFTS
+    def prepare(kind, slot, first, second):
+        rights[kind * UPPER + slot] = jnp.concatenate([as_right(first), as_right(second)], axis=1)
+
+    def multiply(kind, slot):
+        group = kind * UPPER + slot
+        both = product(lower[...], rights[group]).reshape(LEFTS, BLOCK, 2 * BLOCK)
+        start = group * 2 * LEFTS
         products[pl.ds(start, LEFTS)] = both[:, :, :BLOCK]
         products[pl.ds(start + LEFTS, LEFTS)] = both[:, :, BLOCK:]
 
-    def multiply_halo(sweep, *steps):
+    def arrive(sweep, *steps):
         for kind, slot in steps:
-            for e in range(2):
-                transfer(sweep, kind, e, slot).wait_recv()
+            wait_arrived(sweep, kind, slot)
         for kind, slot in steps:
-            multiply(kind, slot, halo[sweep, kind - 1, slot, 0], halo[sweep, kind - 1, slot, 1])
-
-    def wait_sent(sweep, slots):
-        for slot in slots:
-            for kind in (FIRST, SECOND):
-                for e in range(2):
-                    @pl.when(exists[kind][e])
-                    def _():
-                        transfer(sweep, kind, e, slot).wait_send()
+            prepare(kind, slot, halo[sweep, kind - 1, slot, 0], halo[sweep, kind - 1, slot, 1])
+
+    def own(sweep, row, slot):
+        return held[row, LOWER + slot] if sweep == 0 else upper[row, slot]
+
+    def invert(sweep, *kinds):
+        squares = []
+        for kind in kinds:
+            if kind == OWN:
+                squares += [own(sweep, row, 0) for row in range(ROWS)]
+            else:
+                squares += [halo[sweep, kind - 1, 0, e] for e in range(2)]
+        for index, inverse in enumerate(newton_inverses(squares)):
+            inverses[kinds[0] * 2 + index] = as_right(inverse)
 
     def fill(sweep):
-        def own(row, slot):
-            return held[row, LOWER + slot] if sweep == 0 else upper[row, slot]
-
         for slot in range(UPPER):
-            multiply(OWN, slot, own(0, slot), own(1, slot))
-        if sweep == 1:
-            wait_sent(0, range(UPPER))
-        multiply_halo(sweep, (FIRST, 0), (SECOND, 0))
-        squares = [own(0, 0), own(1, 0)]
-        for kind in (FIRST, SECOND):
-            squares += [halo[sweep, kind - 1, 0, e] for e in range(2)]
-        for index, inverse in enumerate(newton_inverses(squares)):
-            inverses[index] = as_right(inverse)
-        multiply_halo(sweep, (FIRST, 1), (FIRST, 2), (SECOND, 1))
-        multiply_halo(sweep, (FIRST, 3), (SECOND, 2))
-        if sweep == 1:
-            wait_sent(1, range(UPPER - 1))
-        multiply_halo(sweep, (SECOND, 3))
+            prepare(OWN, slot, own(sweep, 0, slot), own(sweep, 1, slot))
+        for slot in range(UPPER):
+            multiply(OWN, slot)
+        invert(sweep, OWN)
+        arrive(sweep, (FIRST, 0), (SECOND, 0))
+        multiply(FIRST, 0)
+        multiply(SECOND, 0)
+        invert(sweep, FIRST, SECOND)
+        arrive(sweep, (FIRST, 1), (SECOND, 1))
+        multiply(FIRST, 1)
+        multiply(SECOND, 1)
+        arrive(sweep, (FIRST, 2), (SECOND, 2))
+        multiply(FIRST, 2)
+        multiply(SECOND, 2)
+        arrive(sweep, (FIRST, 3), (SECOND, 3))
+        multiply(FIRST, 3)
+        multiply(SECOND, 3)
 
     def residue(row, slot):
         target = (row * SLOTS + slot) * PAIRS
@@ -225,10 +249,7 @@
         for slot in slots:
             for row in range(ROWS):
                 upper[row, slot] = residue(row, LOWER + slot)
-        for slot in slots:
-            for kind in (SECOND, FIRST):
-                for e in range(2):
-                    start(1, kind, e, slot)
+        send(1, slots)
     for index in range(LEFTS):
         lower[pl.ds(index * BLOCK, BLOCK)] = as_left(lower_block(index))
 
@@ -238,7 +259,7 @@
     for slot in range(UPPER):
         for row in range(ROWS):
             out_ref[row, LOWER + slot] = residue(row, LOWER + slot)
-    wait_sent(1, (UPPER - 1,))
+    wait_sent()
 
 
 def local(matrix, left_slots, right_rows, right_slots, pair_counts, diag_rows):
@@ -258,6 +279,7 @@
             pltpu.SMEM((ROWS, LOWER), jnp.int32),
             pltpu.VMEM((ROWS, SLOTS, BLOCK, BLOCK), F32),
             pltpu.VMEM((LEFTS * BLOCK, 3 * BLOCK), BF16),
+            pltpu.VMEM((3 * UPPER, 3 * BLOCK, 2 * BLOCK), BF16),
             pltpu.VMEM((ROWS, UPPER, BLOCK, BLOCK), F32),
             pltpu.VMEM((2, 2, UPPER, 2, BLOCK, BLOCK), F32),
             pltpu.VMEM((WINDOW * LEFTS + 1, BLOCK, BLOCK), F32),
@@ -266,8 +288,8 @@
             pltpu.SMEM((LEFTS,), jnp.int32),
             pltpu.SemaphoreType.DMA,
             pltpu.SemaphoreType.DMA((5,)),
-            pltpu.SemaphoreType.DMA((2, 2, UPPER, 2)),
-            pltpu.SemaphoreType.DMA((2, 2, UPPER, 2)),
+            pltpu.SemaphoreType.DMA((2, 2)),
+            pltpu.SemaphoreType.DMA((2, 2, UPPER)),
         ],
         compiler_params=pltpu.CompilerParams(
             collective_id=0, has_side_effects=True, vmem_limit_bytes=48 * 2**20

time: 26 us -> 25.4 us (0.977)
  the two profiles are of different devices: /device:TPU:168 before, /device:TPU:159 now
where the time goes in v2:
time: 25.4 us; the launch traced here: 25.2 us
  Pallas kernels  24.3 us (96%)
  local copies, waits for them, and re-layouts  0.97 us (4%)
    pallas_call x1, Pallas kernels, local(): pl.pallas_call(kernel, out_shape=pltpu.VMEM(matrix.shape, F32), in_specs=...  24.3 us
    unnamed x1, local copies, waits for them, and re-layouts  0.97 us

profile of v2, /device:TPU:159, one launch (start us, length us, event | category | flops | bytes accessed | tf_op | source)
XLA Modules:
  0.0 25.2 jit_solution(5767965306785146744)
XLA Ops:
  0.0 24.3 %shard_map.64 = f32[2,8,128,128]{3,2,1,0:T(8,128)S(1)} custom-call(f32[2,8,128,128]{3,2,1,0:T(8,128)} %matrix_ref.1, s32[2,4,8]{2,1,0:T(4,128)} %bitcast.3, s32[2,4,8]{2,1,0:T(4,128)} %bitcast.4, s32[2,4,8]{2,1,0:T(4,128)} %bitcast.5, s32[2,8]{1,0:T(2,128)} %counts_hbm.1, s32[2,4]{1,0:T(2,128)} %diag_hbm.1), custom_call_target="tpu_custom_call" | custom-call | tf_op jit(solution)/shard_map/pallas_call | solution.py:269
  24.3 1.0 %copy.8 = f32[2,8,128,128]{3,2,1,0:T(8,128)} copy(f32[2,8,128,128]{3,2,1,0:T(8,128)S(1)} %shard_map.64) | data formatting | bytes 2097152

commit v3 on v2

--- a/solution.py
+++ b/solution.py
@@ -87,19 +87,29 @@
             device_id_type=MESH,
         )
 
+    inside = functools.reduce(jnp.logical_and, exists[FIRST] + exists[SECOND])
+
     def send(sweep, slots=range(UPPER)):
-        for kind in (SECOND, FIRST):
-            after, before = exists[kind]
-            for ways, here in (
-                ((0, 1), jnp.logical_and(after, before)),
-                ((0,), jnp.logical_not(before)),
-                ((1,), jnp.logical_not(after)),
-            ):
-                @pl.when(here)
-                def _():
-                    for slot in slots:
-                        for e in ways:
-                            transfer(sweep, kind, e, slot).start()
+        def start(kind, ways):
+            for slot in slots:
+                for e in ways:
+                    transfer(sweep, kind, e, slot).start()
+
+        @pl.when(inside)
+        def _():
+            for kind in (SECOND, FIRST):
+                start(kind, (0, 1))
+
+        @pl.when(jnp.logical_not(inside))
+        def _():
+            for kind in (SECOND, FIRST):
+                after, before = exists[kind]
+                for ways, here in (
+                    ((0, 1), jnp.logical_and(after, before)),
+                    ((0,), jnp.logical_not(before)),
+                    ((1,), jnp.logical_not(after)),
+                ):
+                    pl.when(here)(functools.partial(start, kind, ways))
 
     def wait_arrived(sweep, kind, slot):
         place = halo.at[sweep, kind - 1, slot]
@@ -245,11 +255,10 @@
         return product(as_left(residue(row, slot)), inverses[diag_places[index]])
 
     fill(0)
-    for slots in ((0,), (1, 2, 3)):
-        for slot in slots:
-            for row in range(ROWS):
-                upper[row, slot] = residue(row, LOWER + slot)
-        send(1, slots)
+    for slot in range(UPPER):
+        for row in range(ROWS):
+            upper[row, slot] = residue(row, LOWER + slot)
+    send(1)
     for index in range(LEFTS):
         lower[pl.ds(index * BLOCK, BLOCK)] = as_left(lower_block(index))
 

time: 25.4 us -> 25.5 us (level)
  no operation moved by 1% of the time
where the time goes in v3:
time: 25.5 us; the launch traced here: 25.4 us
  Pallas kernels  24.4 us (96%)
  local copies, waits for them, and re-layouts  0.97 us (4%)
    pallas_call x1, Pallas kernels, local(): pl.pallas_call(kernel, out_shape=pltpu.VMEM(matrix.shape, F32), in_specs=...  24.4 us
    unnamed x1, local copies, waits for them, and re-layouts  0.97 us

profile of v3, /device:TPU:159, one launch (start us, length us, event | category | flops | bytes accessed | tf_op | source)
XLA Modules:
  0.0 25.4 jit_solution(1028411631604699539)
XLA Ops:
  0.0 24.4 %shard_map.64 = f32[2,8,128,128]{3,2,1,0:T(8,128)S(1)} custom-call(f32[2,8,128,128]{3,2,1,0:T(8,128)} %matrix_ref.1, s32[2,4,8]{2,1,0:T(4,128)} %bitcast.3, s32[2,4,8]{2,1,0:T(4,128)} %bitcast.4, s32[2,4,8]{2,1,0:T(4,128)} %bitcast.5, s32[2,8]{1,0:T(2,128)} %counts_hbm.1, s32[2,4]{1,0:T(2,128)} %diag_hbm.1), custom_call_target="tpu_custom_call" | custom-call | tf_op jit(solution)/shard_map/pallas_call | solution.py:278
  24.4 1.0 %copy.8 = f32[2,8,128,128]{3,2,1,0:T(8,128)} copy(f32[2,8,128,128]{3,2,1,0:T(8,128)S(1)} %shard_map.64) | data formatting | bytes 2097152
